TPU v7x, 256 devices: a whole 4x4x8 slice. The times are simulated.
256 devices in a mesh: wide: 32 (over y_lo, z, core), narrow: 8 (over y_hi, x).
Axes of the slice: x: 4, y: 4 (y_hi: 2, y_lo: 2; y = y_hi * 2 + y_lo), z: 8, core: 2. Of those that a mesh axis runs over, the one named last changes fastest.
Arguments:
- mentions: bfloat16 [16384, 768], P('wide'), may hold values from -16 to 16
- gold_vectors: bfloat16 [16384, 768], P('wide'), may hold values from -2 to 2
- gold_ids: int32 [16384], P('wide'), may hold values from 0 to 511
- cache: bfloat16 [32768, 768], P(('wide', 'narrow')), may hold values from -4 to 4
- cache_ids: int32 [32768], P(('wide', 'narrow')), may hold values from 0 to 511
Outputs:
- loss: float32 [16384], P('wide')
- mention_grad: float32 [16384, 768], P(('wide', 'narrow'))
All inputs are finite; a program needn't handle non-finite values.
Results may differ from a plain program's by a relative error of at most 0.0015.
Values may be sent and summed in bfloat16 or wider, within the bound.
A program may use at most 64 MiB of HBM per device.

v0:
```python
import jax
import jax.numpy as jnp
from jax import lax
from jax.sharding import PartitionSpec as P

NEG = -1e30


def passed_along(value, axis, steps):
    count = lax.axis_size(axis)
    pairs = [(source, (source + steps) % count) for source in range(count)]
    return lax.ppermute(value, axis, pairs)


def block_scores(block, mentions):
    return lax.dot_general(
        block, mentions, (((1,), (1,)), ((), ())), preferred_element_type=jnp.float32
    )


def forward_piece(state, kept, block, ids, mentions, gold_ids):
    scores = block_scores(block, mentions)
    allowed = ids[:, None] != gold_ids[None, :]
    running, total = state
    block_top = jnp.max(jnp.where(allowed, scores, NEG), axis=0)
    newest = jnp.maximum(running, block_top)
    total = total * jnp.exp(running - newest) + jnp.sum(
        jnp.exp(jnp.where(allowed, scores - newest[None, :], NEG)), axis=0
    )
    return ((newest, total), kept)


def backward_piece(grad, block, ids, mentions, gold_ids, lse):
    scores = block_scores(block, mentions)
    allowed = ids[:, None] != gold_ids[None, :]
    weights = jnp.exp(jnp.where(allowed, scores - lse[None, :], NEG)).astype(jnp.bfloat16)
    return grad + lax.dot_general(
        weights, block, (((0,), (0,)), ((), ())), preferred_element_type=jnp.float32
    )


def settle(state, gold_score):
    running, total = state
    top_all = lax.pmax(running, "narrow")
    total_all = lax.psum(total * jnp.exp(running - top_all), "narrow")
    highest = jnp.maximum(top_all, gold_score)
    whole = total_all * jnp.exp(top_all - highest) + jnp.exp(gold_score - highest)
    return highest + jnp.log(whole)


def per_device(mentions, gold_vectors, gold_ids, cache, cache_ids):
    width = lax.axis_size("wide")
    count = mentions.shape[0]
    features = mentions.shape[1]
    gold_score = jnp.sum(mentions.astype(jnp.float32) * gold_vectors.astype(jnp.float32), axis=1)
    state = (jnp.full((count,), NEG, jnp.float32), jnp.zeros((count,), jnp.float32))
    kept = jnp.zeros((1, 1), jnp.float32)
    grad = jnp.zeros((count, features), jnp.float32)

    def cycle_forward(step, carry):
        block, ids, inner, stored = carry
        inner, stored = forward_piece(inner, stored, block, ids, mentions, gold_ids)
        block, ids = passed_along((block, ids), "wide", 1)
        return (block, ids, inner, stored)

    block, ids, state, kept = lax.fori_loop(
        0, width - 1, cycle_forward, (cache, cache_ids, state, kept)
    )
    state, kept = forward_piece(state, kept, block, ids, mentions, gold_ids)
    lse = settle(state, gold_score)

    def cycle_backward(step, carry):
        block, ids, total = carry
        total = backward_piece(total, block, ids, mentions, gold_ids, lse)
        block, ids = passed_along((block, ids), "wide", 1)
        return (block, ids, total)

    block, ids, grad = lax.fori_loop(0, width - 1, cycle_backward, (cache, cache_ids, grad))
    grad = backward_piece(grad, block, ids, mentions, gold_ids, lse)
    loss = lse - gold_score
    share = lax.psum_scatter(grad, "narrow", scatter_dimension=0, tiled=True)
    part_rows = share.shape[0]
    offset = lax.axis_index("narrow") * part_rows
    gold_part = lax.dynamic_slice_in_dim(gold_score, offset, part_rows, 0)
    lse_part = lax.dynamic_slice_in_dim(lse, offset, part_rows, 0)
    vector_part = lax.dynamic_slice_in_dim(gold_vectors, offset, part_rows, 0).astype(jnp.float32)
    mention_grad = share + (jnp.exp(gold_part - lse_part) - 1.0)[:, None] * vector_part
    return (loss, mention_grad)


def solution(mesh):
    in_specs = (
        P("wide", None),
        P("wide", None),
        P("wide"),
        P(("wide", "narrow"), None),
        P(("wide", "narrow")),
    )
    out_specs = (P("wide"), P(("wide", "narrow"), None))
    return jax.shard_map(
        per_device, mesh=mesh, in_specs=in_specs, out_specs=out_specs, check_vma=False
    )
```

profile of v0, /device:TPU:1, one launch (start us, length us, event | category | flops | bytes accessed | tf_op | source)
XLA Modules:
  0.0 593.0 jit_solution(15642892044390864570)
XLA Ops:
  10.6 224.3 %while.32 = (s32[]{:T(128)}, bf16[128,768]{1,0:T(8,128)(2,1)S(1)}, s32[128]{0:T(128)S(1)}, f32[512]{0:T(512)S(1)}, f32[512]{0:T(512)S(1)}, /*index=5*/s32[512]{0...) while((s32[]{:T(128)}, bf16[128,768]{1,0:T(8,128)(2,1)S(1)}, s32[128]{0:T(128)S(1)}, ...), condition=%wide.region_3.0_spmd.clone, body=%wide.region_0.3_spmd.clone.sunk | while | flops 101124608 | bytes 2721976 | solution.py:66
  38.3 6.2 %collective-permute-done.1 = s32[128]{0:T(128)S(1)} collective-permute-done((s32[128]{0:T(128)S(1)}, s32[128]{0:T(128)S(1)}, u32[]{:S(2)}, u32[]{:S(2)}) %collective-permute-start.1) | collective-permute-done | bytes 544 | tf_op jit(solution)/shard_map/while/body/eval_jaxpr/ppermute | solution.py:12
  45.6 6.2 %collective-permute-done.1 = s32[128]{0:T(128)S(1)} collective-permute-done((s32[128]{0:T(128)S(1)}, s32[128]{0:T(128)S(1)}, u32[]{:S(2)}, u32[]{:S(2)}) %collective-permute-start.1) | collective-permute-done | bytes 544 | tf_op jit(solution)/shard_map/while/body/eval_jaxpr/ppermute | solution.py:12
  52.9 6.2 %collective-permute-done.1 = s32[128]{0:T(128)S(1)} collective-permute-done((s32[128]{0:T(128)S(1)}, s32[128]{0:T(128)S(1)}, u32[]{:S(2)}, u32[]{:S(2)}) %collective-permute-start.1) | collective-permute-done | bytes 544 | tf_op jit(solution)/shard_map/while/body/eval_jaxpr/ppermute | solution.py:12
  67.5 6.2 %collective-permute-done.1 = s32[128]{0:T(128)S(1)} collective-permute-done((s32[128]{0:T(128)S(1)}, s32[128]{0:T(128)S(1)}, u32[]{:S(2)}, u32[]{:S(2)}) %collective-permute-start.1) | collective-permute-done | bytes 544 | tf_op jit(solution)/shard_map/while/body/eval_jaxpr/ppermute | solution.py:12
  74.8 6.2 %collective-permute-done.1 = s32[128]{0:T(128)S(1)} collective-permute-done((s32[128]{0:T(128)S(1)}, s32[128]{0:T(128)S(1)}, u32[]{:S(2)}, u32[]{:S(2)}) %collective-permute-start.1) | collective-permute-done | bytes 544 | tf_op jit(solution)/shard_map/while/body/eval_jaxpr/ppermute | solution.py:12
  96.8 6.2 %collective-permute-done.1 = s32[128]{0:T(128)S(1)} collective-permute-done((s32[128]{0:T(128)S(1)}, s32[128]{0:T(128)S(1)}, u32[]{:S(2)}, u32[]{:S(2)}) %collective-permute-start.1) | collective-permute-done | bytes 544 | tf_op jit(solution)/shard_map/while/body/eval_jaxpr/ppermute | solution.py:12
  104.1 6.2 %collective-permute-done.1 = s32[128]{0:T(128)S(1)} collective-permute-done((s32[128]{0:T(128)S(1)}, s32[128]{0:T(128)S(1)}, u32[]{:S(2)}, u32[]{:S(2)}) %collective-permute-start.1) | collective-permute-done | bytes 544 | tf_op jit(solution)/shard_map/while/body/eval_jaxpr/ppermute | solution.py:12
  126.0 6.2 %collective-permute-done.1 = s32[128]{0:T(128)S(1)} collective-permute-done((s32[128]{0:T(128)S(1)}, s32[128]{0:T(128)S(1)}, u32[]{:S(2)}, u32[]{:S(2)}) %collective-permute-start.1) | collective-permute-done | bytes 544 | tf_op jit(solution)/shard_map/while/body/eval_jaxpr/ppermute | solution.py:12
  133.3 6.2 %collective-permute-done.1 = s32[128]{0:T(128)S(1)} collective-permute-done((s32[128]{0:T(128)S(1)}, s32[128]{0:T(128)S(1)}, u32[]{:S(2)}, u32[]{:S(2)}) %collective-permute-start.1) | collective-permute-done | bytes 544 | tf_op jit(solution)/shard_map/while/body/eval_jaxpr/ppermute | solution.py:12
  140.6 6.2 %collective-permute-done.1 = s32[128]{0:T(128)S(1)} collective-permute-done((s32[128]{0:T(128)S(1)}, s32[128]{0:T(128)S(1)}, u32[]{:S(2)}, u32[]{:S(2)}) %collective-permute-start.1) | collective-permute-done | bytes 544 | tf_op jit(solution)/shard_map/while/body/eval_jaxpr/ppermute | solution.py:12
  155.2 6.2 %collective-permute-done.1 = s32[128]{0:T(128)S(1)} collective-permute-done((s32[128]{0:T(128)S(1)}, s32[128]{0:T(128)S(1)}, u32[]{:S(2)}, u32[]{:S(2)}) %collective-permute-start.1) | collective-permute-done | bytes 544 | tf_op jit(solution)/shard_map/while/body/eval_jaxpr/ppermute | solution.py:12
  162.5 6.2 %collective-permute-done.1 = s32[128]{0:T(128)S(1)} collective-permute-done((s32[128]{0:T(128)S(1)}, s32[128]{0:T(128)S(1)}, u32[]{:S(2)}, u32[]{:S(2)}) %collective-permute-start.1) | collective-permute-done | bytes 544 | tf_op jit(solution)/shard_map/while/body/eval_jaxpr/ppermute | solution.py:12
  169.8 6.2 %collective-permute-done.1 = s32[128]{0:T(128)S(1)} collective-permute-done((s32[128]{0:T(128)S(1)}, s32[128]{0:T(128)S(1)}, u32[]{:S(2)}, u32[]{:S(2)}) %collective-permute-start.1) | collective-permute-done | bytes 544 | tf_op jit(solution)/shard_map/while/body/eval_jaxpr/ppermute | solution.py:12
  184.5 6.2 %collective-permute-done.1 = s32[128]{0:T(128)S(1)} collective-permute-done((s32[128]{0:T(128)S(1)}, s32[128]{0:T(128)S(1)}, u32[]{:S(2)}, u32[]{:S(2)}) %collective-permute-start.1) | collective-permute-done | bytes 544 | tf_op jit(solution)/shard_map/while/body/eval_jaxpr/ppermute | solution.py:12
  191.8 6.2 %collective-permute-done.1 = s32[128]{0:T(128)S(1)} collective-permute-done((s32[128]{0:T(128)S(1)}, s32[128]{0:T(128)S(1)}, u32[]{:S(2)}, u32[]{:S(2)}) %collective-permute-start.1) | collective-permute-done | bytes 544 | tf_op jit(solution)/shard_map/while/body/eval_jaxpr/ppermute | solution.py:12
  213.7 6.2 %collective-permute-done.1 = s32[128]{0:T(128)S(1)} collective-permute-done((s32[128]{0:T(128)S(1)}, s32[128]{0:T(128)S(1)}, u32[]{:S(2)}, u32[]{:S(2)}) %collective-permute-start.1) | collective-permute-done | bytes 544 | tf_op jit(solution)/shard_map/while/body/eval_jaxpr/ppermute | solution.py:12
  221.0 6.2 %collective-permute-done.1 = s32[128]{0:T(128)S(1)} collective-permute-done((s32[128]{0:T(128)S(1)}, s32[128]{0:T(128)S(1)}, u32[]{:S(2)}, u32[]{:S(2)}) %collective-permute-start.1) | collective-permute-done | bytes 544 | tf_op jit(solution)/shard_map/while/body/eval_jaxpr/ppermute | solution.py:12
  228.3 6.2 %collective-permute-done.1 = s32[128]{0:T(128)S(1)} collective-permute-done((s32[128]{0:T(128)S(1)}, s32[128]{0:T(128)S(1)}, u32[]{:S(2)}, u32[]{:S(2)}) %collective-permute-start.1) | collective-permute-done | bytes 544 | tf_op jit(solution)/shard_map/while/body/eval_jaxpr/ppermute | solution.py:12
  235.3 20.3 %pmax.7 = f32[512]{0:T(512)S(1)} all-reduce(f32[512]{0:T(512)S(1)} %max.11), channel_id=1, replica_groups=mesh['wide'=32,'narrow'=8] {'narrow'}, use_global_device_ids=true, to_apply=%region_5.6 | all-reduce | flops 512 | bytes 4096 | tf_op jit(solution)/shard_map/pmax | solution.py:44
  255.7 15.7 %psum.7 = f32[512]{0:T(512)S(1)} all-reduce(f32[512]{0:T(512)S(1)} %exponential_multiply_fusion), channel_id=1, replica_groups=mesh['wide'=32,'narrow'=8] {'narrow'}, use_global_device_ids=true, to_apply=%region_8.9 | all-reduce | flops 512 | bytes 4096 | tf_op jit(solution)/shard_map/psum | solution.py:45
  272.0 233.6 %while.33 = (s32[]{:T(128)}, bf16[128,768]{1,0:T(8,128)(2,1)S(1)}, s32[128]{0:T(128)S(1)}, f32[512,768]{1,0:T(8,128)S(1)}, s32[512]{0:T(512)S(1)}, /*index=5*/bf...) while((s32[]{:T(128)}, bf16[128,768]{1,0:T(8,128)(2,1)S(1)}, ...), condition=%wide.region_10.11_spmd.clone, body=%wide.region_9.10_spmd.clone.sunk | while | flops 202375168 | bytes 5316279 | solution.py:78
  278.1 7.8 %collective-permute-done.3 = s32[128]{0:T(128)S(1)} collective-permute-done((s32[128]{0:T(128)S(1)}, s32[128]{0:T(128)S(1)}, u32[]{:S(2)}, u32[]{:S(2)}) %collective-permute-start.3) | collective-permute-done | bytes 544 | tf_op jit(solution)/shard_map/while/body/eval_jaxpr/ppermute | solution.py:12
  507.7 76.7 %reduce-scatter.2.cloned.1.call-done = f32[64,768]{1,0:T(8,128)} async-done(((f32[512,768]{1,0:T(8,128)}), f32[64,768]{1,0:T(8,128)}) %reduce-scatter.2.cloned.1.call-update) | async-done | bytes 196624 | tf_op jit(solution)/shard_map/reduce_scatter | solution.py:81
  (561 shorter events, 345.1 us)
Async XLA Ops:
  7.2 577.2 %reduce-scatter.2.cloned.1.call-start = ((), (), s32[]{:S(2)}) async-start(), calls=%async_computation.1 | async-start | bytes 1769472 | tf_op jit(solution)/shard_map/reduce_scatter | solution.py:81
  30.3 7.3 %collective-permute-start = (bf16[128,768]{1,0:T(8,128)(2,1)S(1)}, bf16[128,768]{1,0:T(8,128)(2,1)S(1)}, u32[]{:S(2)}, u32[]{:S(2)}) collective-permute-start(bf16[128,768]{1,0:T(8,128)(2,1)S(1)} %copy.13), channel_id=1, source_target_pairs={{0,8},{8,16},{16,24},{24,32},{32,40},{40,48},{48,56},{56,64},{64,7... | collective-permute-start | bytes 589832 | tf_op jit(solution)/shard_map/while/body/eval_jaxpr/ppermute | solution.py:12
  37.6 7.3 %collective-permute-start = (bf16[128,768]{1,0:T(8,128)(2,1)S(1)}, bf16[128,768]{1,0:T(8,128)(2,1)S(1)}, u32[]{:S(2)}, u32[]{:S(2)}) collective-permute-start(bf16[128,768]{1,0:T(8,128)(2,1)S(1)} %copy.13), channel_id=1, source_target_pairs={{0,8},{8,16},{16,24},{24,32},{32,40},{40,48},{48,56},{56,64},{64,7... | collective-permute-start | bytes 589832 | tf_op jit(solution)/shard_map/while/body/eval_jaxpr/ppermute | solution.py:12
  44.9 7.3 %collective-permute-start = (bf16[128,768]{1,0:T(8,128)(2,1)S(1)}, bf16[128,768]{1,0:T(8,128)(2,1)S(1)}, u32[]{:S(2)}, u32[]{:S(2)}) collective-permute-start(bf16[128,768]{1,0:T(8,128)(2,1)S(1)} %copy.13), channel_id=1, source_target_pairs={{0,8},{8,16},{16,24},{24,32},{32,40},{40,48},{48,56},{56,64},{64,7... | collective-permute-start | bytes 589832 | tf_op jit(solution)/shard_map/while/body/eval_jaxpr/ppermute | solution.py:12
  52.2 7.3 %collective-permute-start = (bf16[128,768]{1,0:T(8,128)(2,1)S(1)}, bf16[128,768]{1,0:T(8,128)(2,1)S(1)}, u32[]{:S(2)}, u32[]{:S(2)}) collective-permute-start(bf16[128,768]{1,0:T(8,128)(2,1)S(1)} %copy.13), channel_id=1, source_target_pairs={{0,8},{8,16},{16,24},{24,32},{32,40},{40,48},{48,56},{56,64},{64,7... | collective-permute-start | bytes 589832 | tf_op jit(solution)/shard_map/while/body/eval_jaxpr/ppermute | solution.py:12
  59.5 7.3 %collective-permute-start = (bf16[128,768]{1,0:T(8,128)(2,1)S(1)}, bf16[128,768]{1,0:T(8,128)(2,1)S(1)}, u32[]{:S(2)}, u32[]{:S(2)}) collective-permute-start(bf16[128,768]{1,0:T(8,128)(2,1)S(1)} %copy.13), channel_id=1, source_target_pairs={{0,8},{8,16},{16,24},{24,32},{32,40},{40,48},{48,56},{56,64},{64,7... | collective-permute-start | bytes 589832 | tf_op jit(solution)/shard_map/while/body/eval_jaxpr/ppermute | solution.py:12
  66.9 7.3 %collective-permute-start = (bf16[128,768]{1,0:T(8,128)(2,1)S(1)}, bf16[128,768]{1,0:T(8,128)(2,1)S(1)}, u32[]{:S(2)}, u32[]{:S(2)}) collective-permute-start(bf16[128,768]{1,0:T(8,128)(2,1)S(1)} %copy.13), channel_id=1, source_target_pairs={{0,8},{8,16},{16,24},{24,32},{32,40},{40,48},{48,56},{56,64},{64,7... | collective-permute-start | bytes 589832 | tf_op jit(solution)/shard_map/while/body/eval_jaxpr/ppermute | solution.py:12
  74.2 7.3 %collective-permute-start = (bf16[128,768]{1,0:T(8,128)(2,1)S(1)}, bf16[128,768]{1,0:T(8,128)(2,1)S(1)}, u32[]{:S(2)}, u32[]{:S(2)}) collective-permute-start(bf16[128,768]{1,0:T(8,128)(2,1)S(1)} %copy.13), channel_id=1, source_target_pairs={{0,8},{8,16},{16,24},{24,32},{32,40},{40,48},{48,56},{56,64},{64,7... | collective-permute-start | bytes 589832 | tf_op jit(solution)/shard_map/while/body/eval_jaxpr/ppermute | solution.py:12
  81.5 7.3 %collective-permute-start = (bf16[128,768]{1,0:T(8,128)(2,1)S(1)}, bf16[128,768]{1,0:T(8,128)(2,1)S(1)}, u32[]{:S(2)}, u32[]{:S(2)}) collective-permute-start(bf16[128,768]{1,0:T(8,128)(2,1)S(1)} %copy.13), channel_id=1, source_target_pairs={{0,8},{8,16},{16,24},{24,32},{32,40},{40,48},{48,56},{56,64},{64,7... | collective-permute-start | bytes 589832 | tf_op jit(solution)/shard_map/while/body/eval_jaxpr/ppermute | solution.py:12
  88.8 7.3 %collective-permute-start = (bf16[128,768]{1,0:T(8,128)(2,1)S(1)}, bf16[128,768]{1,0:T(8,128)(2,1)S(1)}, u32[]{:S(2)}, u32[]{:S(2)}) collective-permute-start(bf16[128,768]{1,0:T(8,128)(2,1)S(1)} %copy.13), channel_id=1, source_target_pairs={{0,8},{8,16},{16,24},{24,32},{32,40},{40,48},{48,56},{56,64},{64,7... | collective-permute-start | bytes 589832 | tf_op jit(solution)/shard_map/while/body/eval_jaxpr/ppermute | solution.py:12
  96.1 7.3 %collective-permute-start = (bf16[128,768]{1,0:T(8,128)(2,1)S(1)}, bf16[128,768]{1,0:T(8,128)(2,1)S(1)}, u32[]{:S(2)}, u32[]{:S(2)}) collective-permute-start(bf16[128,768]{1,0:T(8,128)(2,1)S(1)} %copy.13), channel_id=1, source_target_pairs={{0,8},{8,16},{16,24},{24,32},{32,40},{40,48},{48,56},{56,64},{64,7... | collective-permute-start | bytes 589832 | tf_op jit(solution)/shard_map/while/body/eval_jaxpr/ppermute | solution.py:12
  103.4 7.3 %collective-permute-start = (bf16[128,768]{1,0:T(8,128)(2,1)S(1)}, bf16[128,768]{1,0:T(8,128)(2,1)S(1)}, u32[]{:S(2)}, u32[]{:S(2)}) collective-permute-start(bf16[128,768]{1,0:T(8,128)(2,1)S(1)} %copy.13), channel_id=1, source_target_pairs={{0,8},{8,16},{16,24},{24,32},{32,40},{40,48},{48,56},{56,64},{64,7... | collective-permute-start | bytes 589832 | tf_op jit(solution)/shard_map/while/body/eval_jaxpr/ppermute | solution.py:12
  118.0 7.3 %collective-permute-start = (bf16[128,768]{1,0:T(8,128)(2,1)S(1)}, bf16[128,768]{1,0:T(8,128)(2,1)S(1)}, u32[]{:S(2)}, u32[]{:S(2)}) collective-permute-start(bf16[128,768]{1,0:T(8,128)(2,1)S(1)} %copy.13), channel_id=1, source_target_pairs={{0,8},{8,16},{16,24},{24,32},{32,40},{40,48},{48,56},{56,64},{64,7... | collective-permute-start | bytes 589832 | tf_op jit(solution)/shard_map/while/body/eval_jaxpr/ppermute | solution.py:12
  154.5 7.3 %collective-permute-start = (bf16[128,768]{1,0:T(8,128)(2,1)S(1)}, bf16[128,768]{1,0:T(8,128)(2,1)S(1)}, u32[]{:S(2)}, u32[]{:S(2)}) collective-permute-start(bf16[128,768]{1,0:T(8,128)(2,1)S(1)} %copy.13), channel_id=1, source_target_pairs={{0,8},{8,16},{16,24},{24,32},{32,40},{40,48},{48,56},{56,64},{64,7... | collective-permute-start | bytes 589832 | tf_op jit(solution)/shard_map/while/body/eval_jaxpr/ppermute | solution.py:12
  205.7 7.3 %collective-permute-start = (bf16[128,768]{1,0:T(8,128)(2,1)S(1)}, bf16[128,768]{1,0:T(8,128)(2,1)S(1)}, u32[]{:S(2)}, u32[]{:S(2)}) collective-permute-start(bf16[128,768]{1,0:T(8,128)(2,1)S(1)} %copy.13), channel_id=1, source_target_pairs={{0,8},{8,16},{16,24},{24,32},{32,40},{40,48},{48,56},{56,64},{64,7... | collective-permute-start | bytes 589832 | tf_op jit(solution)/shard_map/while/body/eval_jaxpr/ppermute | solution.py:12
  272.0 13.9 %collective-permute-start.3 = (s32[128]{0:T(128)S(1)}, s32[128]{0:T(128)S(1)}, u32[]{:S(2)}, u32[]{:S(2)}) collective-permute-start(s32[128]{0:T(128)S(1)} %copy.28), channel_id=1, source_target_pairs={{0,8},{8,16},{16,24},{24,32},{32,40},{40,48},{48,56},{56,64},{64,7... | collective-permute-start | bytes 1544 | tf_op jit(solution)/shard_map/while/body/eval_jaxpr/ppermute | solution.py:12
  277.0 9.4 %collective-permute-start.2 = (bf16[128,768]{1,0:T(8,128)(2,1)S(1)}, bf16[128,768]{1,0:T(8,128)(2,1)S(1)}, u32[]{:S(2)}, u32[]{:S(2)}) collective-permute-start(bf16[128,768]{1,0:T(8,128)(2,1)S(1)} %copy.27), channel_id=1, source_target_pairs={{0,8},{8,16},{16,24},{24,32},{32,40},{40,48},{48,56},{56,64},{64,7... | collective-permute-start | bytes 589832 | tf_op jit(solution)/shard_map/while/body/eval_jaxpr/ppermute | solution.py:12
  286.4 7.3 %collective-permute-start.2 = (bf16[128,768]{1,0:T(8,128)(2,1)S(1)}, bf16[128,768]{1,0:T(8,128)(2,1)S(1)}, u32[]{:S(2)}, u32[]{:S(2)}) collective-permute-start(bf16[128,768]{1,0:T(8,128)(2,1)S(1)} %copy.27), channel_id=1, source_target_pairs={{0,8},{8,16},{16,24},{24,32},{32,40},{40,48},{48,56},{56,64},{64,7... | collective-permute-start | bytes 589832 | tf_op jit(solution)/shard_map/while/body/eval_jaxpr/ppermute | solution.py:12
  322.9 7.3 %collective-permute-start.2 = (bf16[128,768]{1,0:T(8,128)(2,1)S(1)}, bf16[128,768]{1,0:T(8,128)(2,1)S(1)}, u32[]{:S(2)}, u32[]{:S(2)}) collective-permute-start(bf16[128,768]{1,0:T(8,128)(2,1)S(1)} %copy.27), channel_id=1, source_target_pairs={{0,8},{8,16},{16,24},{24,32},{32,40},{40,48},{48,56},{56,64},{64,7... | collective-permute-start | bytes 589832 | tf_op jit(solution)/shard_map/while/body/eval_jaxpr/ppermute | solution.py:12
  359.5 7.3 %collective-permute-start.2 = (bf16[128,768]{1,0:T(8,128)(2,1)S(1)}, bf16[128,768]{1,0:T(8,128)(2,1)S(1)}, u32[]{:S(2)}, u32[]{:S(2)}) collective-permute-start(bf16[128,768]{1,0:T(8,128)(2,1)S(1)} %copy.27), channel_id=1, source_target_pairs={{0,8},{8,16},{16,24},{24,32},{32,40},{40,48},{48,56},{56,64},{64,7... | collective-permute-start | bytes 589832 | tf_op jit(solution)/shard_map/while/body/eval_jaxpr/ppermute | solution.py:12
  374.1 7.3 %collective-permute-start.2 = (bf16[128,768]{1,0:T(8,128)(2,1)S(1)}, bf16[128,768]{1,0:T(8,128)(2,1)S(1)}, u32[]{:S(2)}, u32[]{:S(2)}) collective-permute-start(bf16[128,768]{1,0:T(8,128)(2,1)S(1)} %copy.27), channel_id=1, source_target_pairs={{0,8},{8,16},{16,24},{24,32},{32,40},{40,48},{48,56},{56,64},{64,7... | collective-permute-start | bytes 589832 | tf_op jit(solution)/shard_map/while/body/eval_jaxpr/ppermute | solution.py:12
  410.6 7.3 %collective-permute-start.2 = (bf16[128,768]{1,0:T(8,128)(2,1)S(1)}, bf16[128,768]{1,0:T(8,128)(2,1)S(1)}, u32[]{:S(2)}, u32[]{:S(2)}) collective-permute-start(bf16[128,768]{1,0:T(8,128)(2,1)S(1)} %copy.27), channel_id=1, source_target_pairs={{0,8},{8,16},{16,24},{24,32},{32,40},{40,48},{48,56},{56,64},{64,7... | collective-permute-start | bytes 589832 | tf_op jit(solution)/shard_map/while/body/eval_jaxpr/ppermute | solution.py:12
  461.8 7.3 %collective-permute-start.2 = (bf16[128,768]{1,0:T(8,128)(2,1)S(1)}, bf16[128,768]{1,0:T(8,128)(2,1)S(1)}, u32[]{:S(2)}, u32[]{:S(2)}) collective-permute-start(bf16[128,768]{1,0:T(8,128)(2,1)S(1)} %copy.27), channel_id=1, source_target_pairs={{0,8},{8,16},{16,24},{24,32},{32,40},{40,48},{48,56},{56,64},{64,7... | collective-permute-start | bytes 589832 | tf_op jit(solution)/shard_map/while/body/eval_jaxpr/ppermute | solution.py:12
  498.3 7.3 %collective-permute-start.2 = (bf16[128,768]{1,0:T(8,128)(2,1)S(1)}, bf16[128,768]{1,0:T(8,128)(2,1)S(1)}, u32[]{:S(2)}, u32[]{:S(2)}) collective-permute-start(bf16[128,768]{1,0:T(8,128)(2,1)S(1)} %copy.27), channel_id=1, source_target_pairs={{0,8},{8,16},{16,24},{24,32},{32,40},{40,48},{48,56},{56,64},{64,7... | collective-permute-start | bytes 589832 | tf_op jit(solution)/shard_map/while/body/eval_jaxpr/ppermute | solution.py:12
  (103 other events, 705.4 us)
Sparse Core Ops, SparseCore 0:
  507.7 76.5 reduce-scatter.1
where the time goes:
time: 593 us
  waiting for transfers between devices  465 us (78%)
  matrix products  47.1 us (8%)
  blocking collectives  36 us (6%)
  starting transfers between devices  17 us (3%)
  between operations  14.1 us (2%)
  other arithmetic  9.13 us (2%)
    ppermute x124, waiting for transfers between devices, passed_along(): return lax.ppermute(value, axis, pairs)  388 us
    reduce_scatter x1, waiting for transfers between devices, per_device(): share = lax.psum_scatter(grad, 'narrow', scatter_dimension=0, tiled=True)  76.7 us
    dot_general x32, matrix products, backward_piece(): lax.dot_general(weights, block, (((0,), (0,)), ((), ())), preferred_eleme...  34.1 us
    pmax x1, blocking collectives, settle(): top_all = lax.pmax(running, 'narrow')  20.3 us
    ppermute x124, starting transfers between devices, passed_along(): return lax.ppermute(value, axis, pairs)  17 us
    psum x1, blocking collectives, settle(): total_all = lax.psum(total * jnp.exp(running - top_all), 'narrow')  15.7 us
    dot_general x32, matrix products, block_scores(): lax.dot_general(block, mentions, (((1,), (1,)), ((), ())), preferred_elem...  13 us
  transfers between devices with their start and end apart: 125, of which 125 were waited for; matrix products, arithmetic and copies ran while one was open for 9% of the time, Pallas kernels for 0%

commit v1 on v0

v1 whole, which is shorter than its diff:
```python
import functools

import jax
import jax.numpy as jnp
from jax import lax
from jax.experimental import pallas as pl
from jax.experimental.pallas import tpu as pltpu
from jax.sharding import PartitionSpec as P

MESH = pl.DeviceIdType.MESH
NEG = -1e30
FLOOR = -1e20
NX, NY, NZ = 4, 4, 8
PIECES = 2
LEVELS = 32766.0
TINY = 1e-35
PEERS = ((2, 1), (1, 1), (3, 1), (2, 0), (0, 1), (1, 0), (3, 0))
ORDER = (0, 8, 1, 2, 9, 10, 3, 4, 11, 12, 5, 6, 13, 14, 7, 15)
EVENTS = (
    (),
    (("y", 0),),
    (("z", 1), ("z", 2)),
    (),
    (("y", 1),),
    (("y", 2),),
    (("z", 3), ("z", 4)),
    (),
    (("y", 3),),
    (("y", 4),),
    (("z", 5), ("z", 6)),
    (),
    (("y", 5),),
    (("z", 7), ("y", 6)),
    (),
    (("y", 7),),
)


def place(x, y, z, c):
    return ((y % 2 * NZ + z) * 2 + c, (y // 2) * NX + x)


def kernel(
    mentions_hbm, gold_hbm, gold_ids_ref, cache_hbm, cache_ids_ref, loss_ref, grad_ref,
    buf, ids, men, gold, gid, gscore, run, low, u, q, rq, stat, rstat, fac, turned,
    local_sem, zs, zr, ys, yr, cs, cr, qs, qr, ss, sr,
):
    w = lax.axis_index("wide")
    n = lax.axis_index("narrow")
    c = w % 2
    z = (w // 2) % NZ
    y = (n // NX) * 2 + w // (2 * NZ)
    x = n % NX
    rows = buf.shape[2]
    piece = rows // PIECES
    part = grad_ref.shape[0]

    up = place(x, y, (z + 1) % NZ, c)
    down = place(x, y, (z + NZ - 1) % NZ, c)
    side = place(x, (y + NY + 1 - 2 * c) % NY, z, c)
    other_side = place(x, (y + NY - 1 + 2 * c) % NY, z, c)
    twin = place(x, y, z, 1 - c)

    def peer(dx, dy, sign):
        return place((x + NX + sign * dx) % NX, (y + 2 * dy) % NY, z, c)

    load_c = pltpu.make_async_copy(cache_hbm, buf.at[0, c], local_sem.at[0])
    load_m = pltpu.make_async_copy(mentions_hbm, men, local_sem.at[1])
    load_g = pltpu.make_async_copy(gold_hbm, gold, local_sem.at[2])
    load_c.start()
    load_m.start()
    load_g.start()
    ids[0, c] = cache_ids_ref[...]

    barrier = pltpu.get_barrier_semaphore()
    sources = [up, down, other_side, twin] + [peer(dx, dy, -1) for dx, dy in PEERS]
    for d in sources:
        pl.semaphore_signal(barrier, inc=1, device_id=d, device_id_type=MESH)

    def moved(src, dst, send, recv, index, core, target, p):
        if p == PIECES:
            source, goal = ids.at[src, core], ids.at[dst, core]
        else:
            s = pl.ds(p * piece, piece)
            source, goal = buf.at[src, core, s], buf.at[dst, core, s]
        return pltpu.make_async_remote_copy(
            src_ref=source, dst_ref=goal, send_sem=send.at[index, p], recv_sem=recv.at[index, p],
            device_id=target, device_id_type=MESH)

    def z_copy(src, dst, target, p):
        return moved(src, dst, zs, zr, dst, c, target, p)

    def y_copy(src, p):
        return moved(src, 8 + src, ys, yr, src, c, side, p)

    def twin_copy(src, p):
        return moved(src, src, cs, cr, src, c, twin, p)

    def twin_arrival(src, p):
        return moved(src, src, cs, cr, src, 1 - c, twin, p)

    def onward(k, p):
        if k == 0:
            z_copy(0, 1, up, p).start()
            z_copy(0, 2, down, p).start()
        elif k in (1, 3):
            z_copy(k, k + 2, up, p).start()
        elif k in (2, 4):
            z_copy(k, k + 2, down, p).start()
        elif k == 5:
            pl.when(c == 0)(lambda: z_copy(5, 7, up, p).start())
        elif k == 6:
            pl.when(c == 1)(lambda: z_copy(6, 7, down, p).start())
        y_copy(k, p).start()
        twin_copy(k, p).start()

    def z_arrived(k, p):
        z_copy(k, k, up, p).wait_recv()

    def y_arrived(k, p):
        y_copy(k, p).wait_recv()

    def handle(events):
        for p in (PIECES,) + tuple(range(PIECES)):
            for kind, k in events:
                if kind == "z":
                    z_arrived(k, p)
                    onward(k, p)
                else:
                    y_arrived(k, p)
                    twin_copy(8 + k, p).start()

    pl.semaphore_wait(barrier, len(sources))
    load_c.wait()
    for p in (PIECES,) + tuple(range(PIECES)):
        onward(0, p)

    run[...] = jnp.full(run.shape, FLOOR, jnp.float32)
    low[...] = jnp.zeros(low.shape, jnp.float32)
    u[...] = jnp.zeros(u.shape, jnp.float32)
    fac[...] = jnp.zeros(fac.shape, jnp.float32)
    blocks = men.shape[0] // 128
    for b in range(blocks):
        row = jnp.broadcast_to(gold_ids_ref[pl.ds(b, 1), :].astype(jnp.float32), (128, 128))
        gid[pl.ds(b * 128, 128), :] = row.T
    load_m.wait()
    load_g.wait()

    def gold_block(b, _):
        s = pl.ds(pl.multiple_of(b * 128, 128), 128)
        both = men[s, :].astype(jnp.float32) * gold[s, :].astype(jnp.float32)
        score = jnp.broadcast_to(jnp.sum(both, axis=1, keepdims=True), (128, 128))
        gscore[pl.ds(b, 1), :] = score.T[0:1, :]
        return 0

    lax.fori_loop(0, blocks, gold_block, 0)

    def step(j, _):
        for i, events in enumerate(EVENTS):
            if events:
                pl.when(j == i)(functools.partial(handle, events))
        slot = jnp.int32(ORDER[0])
        for i in range(1, len(ORDER)):
            slot = jnp.where(j == i, ORDER[i], slot)
        for p in range(PIECES + 1):
            twin_arrival(slot, p).wait_recv()
        block = jnp.concatenate([buf[slot, 0], buf[slot, 1]], axis=0)
        scores = lax.dot_general(
            men[...], block, (((1,), (1,)), ((), ())), preferred_element_type=jnp.float32
        )
        owner = gid[...]
        left = jnp.where(ids[slot, 0].astype(jnp.float32) == owner, NEG, scores[:, :128])
        right = jnp.where(ids[slot, 1].astype(jnp.float32) == owner, NEG, scores[:, 128:])
        top = jnp.max(jnp.maximum(left, right), axis=1, keepdims=True)
        before = run[...]
        newest = jnp.maximum(before, top)
        shrink = jnp.exp(before - newest)
        left = jnp.exp(left - newest)
        right = jnp.exp(right - newest)
        run[...] = newest
        low[...] = low[...] * shrink + (left + right)
        weights = jnp.concatenate([left.astype(jnp.bfloat16), right.astype(jnp.bfloat16)], axis=1)
        terms = jnp.dot(weights, block, preferred_element_type=jnp.float32)
        for f in range(0, terms.shape[1], 128):
            u[:, f:f + 128] = u[:, f:f + 128] * shrink + terms[:, f:f + 128]
        return 0

    lax.fori_loop(0, len(ORDER), step, 0)

    lane = lax.broadcasted_iota(jnp.int32, (128, 128), 1)

    def settle_block(b, _):
        s = pl.ds(pl.multiple_of(b * 128, 128), 128)
        size = jnp.maximum(jnp.max(jnp.abs(u[s, :]), axis=1, keepdims=True), TINY)
        total = jnp.sum(low[s, :], axis=1, keepdims=True)
        cols = jnp.where(lane == 0, run[s, :], jnp.where(lane == 1, total, size))
        turn = cols.T
        stat[pl.ds(b, 1), :] = turn[0:1, :]
        stat[pl.ds(blocks + b, 1), :] = turn[1:2, :]
        stat[pl.ds(2 * blocks + b, 1), :] = turn[2:3, :]
        q[s, :] = jnp.round(u[s, :] * (LEVELS / size)).astype(jnp.int32).astype(jnp.int16)
        return 0

    lax.fori_loop(0, blocks, settle_block, 0)

    def peer_row(dx, dy):
        return ((n // NX + dy) % 2) * NX + (x + dx) % NX

    stat_copies, q_copies = [], []
    for e, (dx, dy) in enumerate(PEERS):
        there = peer(dx, dy, 1)
        stat_copies.append(pltpu.make_async_remote_copy(
            src_ref=stat, dst_ref=rstat.at[e], send_sem=ss.at[e], recv_sem=sr.at[e],
            device_id=there, device_id_type=MESH))
        first = pl.multiple_of(peer_row(dx, dy) * part, part)
        q_copies.append(pltpu.make_async_remote_copy(
            src_ref=q.at[pl.ds(first, part)], dst_ref=rq.at[e], send_sem=qs.at[e], recv_sem=qr.at[e],
            device_id=there, device_id_type=MESH))
    for cp in stat_copies:
        cp.start()
    for cp in q_copies:
        cp.start()
    for cp in stat_copies:
        cp.wait_recv()

    golds = gscore[...]
    tops = [stat[0:blocks, :]] + [rstat[e, 0:blocks, :] for e in range(len(PEERS))]
    sums = [stat[blocks:2 * blocks, :]] + [rstat[e, blocks:2 * blocks, :] for e in range(len(PEERS))]
    highest = golds
    for t in tops:
        highest = jnp.maximum(highest, t)
    whole = jnp.exp(golds - highest)
    for t, s in zip(tops, sums):
        whole = whole + s * jnp.exp(t - highest)
    lse = highest + jnp.log(whole)
    loss_ref[...] = lse - golds
    gscore[...] = jnp.exp(golds - lse) - 1.0
    run[0:blocks, :] = lse

    mine = (n * part) // 128
    row = pl.ds(mine, 1)
    my_lse = run[row, :]
    fac[0:1, :] = jnp.exp(stat[row, :] - my_lse)
    fac[1:2, :] = gscore[row, :]
    for e in range(len(PEERS)):
        size = rstat[e, pl.ds(2 * blocks + mine, 1), :] * (1.0 / LEVELS)
        fac[2 + e:3 + e, :] = size * jnp.exp(rstat[e, row, :] - my_lse)
    turned[...] = fac[...].T
    f = turned[pl.ds(pl.multiple_of((n * part) % 128, part), part), :]
    own = pl.ds(pl.multiple_of(n * part, part), part)
    grad_ref[...] = u[own, :] * f[:, 0:1] + gold[own, :].astype(jnp.float32) * f[:, 1:2]
    for e in range(len(PEERS)):
        q_copies[e].wait_recv()
        grad_ref[...] += rq[e].astype(jnp.int32).astype(jnp.float32) * f[:, 2 + e:3 + e]

    for p in range(PIECES + 1):
        for k in range(1, 8):
            z_copy(k, k, up, p).wait_send()
        for k in range(8):
            y_copy(k, p).wait_send()
        for k in range(16):
            twin_copy(k, p).wait_send()
    for cp in stat_copies + q_copies:
        cp.wait_send()


def per_device(mentions, gold_vectors, gold_ids, cache, cache_ids):
    count, features = mentions.shape
    rows = cache.shape[0]
    blocks = count // 128
    part = count // 8
    near = len(PEERS)
    any_ = pl.BlockSpec(memory_space=pl.ANY)
    vmem = pl.BlockSpec(memory_space=pltpu.VMEM)
    dma = pltpu.SemaphoreType.DMA
    loss, grad = pl.pallas_call(
        kernel,
        out_shape=(
            jax.ShapeDtypeStruct((blocks, 128), jnp.float32),
            jax.ShapeDtypeStruct((part, features), jnp.float32),
        ),
        in_specs=[any_, any_, vmem, any_, vmem],
        out_specs=(vmem, vmem),
        scratch_shapes=[
            pltpu.VMEM((16, 2, rows, features), jnp.bfloat16),
            pltpu.VMEM((16, 2, 1, rows), jnp.int32),
            pltpu.VMEM((count, features), jnp.bfloat16),
            pltpu.VMEM((count, features), jnp.bfloat16),
            pltpu.VMEM((count, 128), jnp.float32),
            pltpu.VMEM((blocks, 128), jnp.float32),
            pltpu.VMEM((count, 128), jnp.float32),
            pltpu.VMEM((count, 128), jnp.float32),
            pltpu.VMEM((count, features), jnp.float32),
            pltpu.VMEM((count, features), jnp.int16),
            pltpu.VMEM((near, part, features), jnp.int16),
            pltpu.VMEM((4 * blocks, 128), jnp.float32),
            pltpu.VMEM((near, 4 * blocks, 128), jnp.float32),
            pltpu.VMEM((128, 128), jnp.float32),
            pltpu.VMEM((128, 128), jnp.float32),
            dma((3,)),
            dma((8, PIECES + 1)),
            dma((8, PIECES + 1)),
            dma((8, PIECES + 1)),
            dma((8, PIECES + 1)),
            dma((16, PIECES + 1)),
            dma((16, PIECES + 1)),
            dma((near,)),
            dma((near,)),
            dma((near,)),
            dma((near,)),
        ],
        compiler_params=pltpu.CompilerParams(
            collective_id=0, has_side_effects=True, vmem_limit_bytes=40 * 2**20
        ),
        name="linking",
    )(mentions, gold_vectors, gold_ids.reshape(blocks, 128), cache, cache_ids.reshape(1, rows))
    return loss.reshape(count), grad


def solution(mesh):
    in_specs = (
        P("wide", None),
        P("wide", None),
        P("wide"),
        P(("wide", "narrow"), None),
        P(("wide", "narrow")),
    )
    out_specs = (P("wide"), P(("wide", "narrow"), None))
    return jax.shard_map(
        per_device, mesh=mesh, in_specs=in_specs, out_specs=out_specs, check_vma=False
    )
```

time: 593 us -> 73.5 us (0.12)
  waiting for transfers between devices: 465 us -> 0 us
  Pallas kernels: 0 us -> 67.5 us
  matrix products: 47.1 us -> 0 us
  blocking collectives: 36 us -> 0 us
  starting transfers between devices: 17 us -> 0 us
  between operations: 14.1 us -> 0.66 us
  other arithmetic: 9.13 us -> 0 us
    ppermute x124 -> x0, waiting for transfers between devices: 388 us -> none  [passed_along(): return lax.ppermute(value, axis, pairs)]
    reduce_scatter x1 -> x0, waiting for transfers between devices: 76.7 us -> none  [per_device(): share = lax.psum_scatter(grad, 'narrow', scatter_dimension=0, tiled=True)]
    pallas_call x0 -> x1, Pallas kernels: none -> 67.5 us  [per_device(): pl.pallas_call(kernel, out_shape=(jax.ShapeDtypeStruct((blocks, 128), jnp...]
    dot_general x64 -> x0, matrix products: 47.1 us -> none  [the longest x32 34.1 us: backward_piece(): lax.dot_general(weights, block, (((0,), (0,)), ((), ())), preferred_eleme...]
    pmax x1 -> x0, blocking collectives: 20.3 us -> none  [settle(): top_all = lax.pmax(running, 'narrow')]
    ppermute x124 -> x0, starting transfers between devices: 17 us -> none  [passed_along(): return lax.ppermute(value, axis, pairs)]
    psum x1 -> x0, blocking collectives: 15.7 us -> none  [settle(): total_all = lax.psum(total * jnp.exp(running - top_all), 'narrow')]
  transfers between devices with their start and end apart: 125 -> 0, of which waited for: 125 -> 0; matrix products, arithmetic and copies ran while one was open for 9% -> 0% of each run, Pallas kernels for 0% -> 0%
where the time goes in v1:
time: 73.5 us; the launch traced here: 73.3 us
  Pallas kernels  67.5 us (92%)
  local copies, waits for them, and re-layouts  5.12 us (7%)
    pallas_call x1, Pallas kernels, per_device(): pl.pallas_call(kernel, out_shape=(jax.ShapeDtypeStruct((blocks, 128), jnp...  67.5 us
    unnamed x12, local copies, waits for them, and re-layouts  5.12 us

profile of v1, /device:TPU:1, one launch (start us, length us, event | category | flops | bytes accessed | tf_op | source)
XLA Modules:
  0.0 73.3 jit_solution(10120856270066052475)
XLA Ops:
  0.6 0.0 copy-start.3
  0.6 0.0 copy-start.4
  0.7 0.7 copy-done.3
  1.3 0.0 copy-done.4
  1.3 0.0 copy-start
  1.3 1.1 %copy-done = bf16[512,768]{1,0:T(8,128)(2,1)S(1)} copy-done((bf16[512,768]{1,0:T(8,128)(2,1)S(1)}, bf16[512,768]{1,0:T(8,128)(2,1)}, u32[]{:S(2)}) %copy-start) | copy-done | bytes 786456
  2.5 0.0 copy-start.1
  2.5 1.1 %copy-done.1 = bf16[512,768]{1,0:T(8,128)(2,1)S(1)} copy-done((bf16[512,768]{1,0:T(8,128)(2,1)S(1)}, bf16[512,768]{1,0:T(8,128)(2,1)}, u32[]{:S(2)}) %copy-start.1) | copy-done | bytes 786456
  3.6 0.0 copy-start.2
  3.6 0.9 %copy-done.2 = bf16[128,768]{1,0:T(8,128)(2,1)S(1)} copy-done((bf16[128,768]{1,0:T(8,128)(2,1)S(1)}, bf16[128,768]{1,0:T(8,128)(2,1)}, u32[]{:S(2)}) %copy-start.2) | copy-done | bytes 196632
  4.5 67.5 %linking.1 = (f32[4,128]{1,0:T(4,128)S(1)}, f32[64,768]{1,0:T(8,128)S(1)}) custom-call(bf16[512,768]{1,0:T(8,128)(2,1)S(1)} %copy-done, bf16[512,768]{1,0:T(8,128)(2,1)S(1)} %copy-done.1, s32[4,128]{1,0:T(4,128)S(1)} %bitcast.3, bf16[128,768]{1,0:T(8,128)(2,1)S(1)} %copy-done.2, s32[1,128]{1,0:T(1,128)S(1)} %bitcast.5), custom_call_target="tpu_custom_call" | custom-call | tf_op jit(solution)/shard_map/linking/pallas_call | solution.py:276
  72.0 0.6 copy.9
  72.6 0.7 copy.10
Async XLA Ops:
  0.6 0.7 copy-start.3
  0.6 0.7 copy-start.4
  1.3 1.1 %copy-start = (bf16[512,768]{1,0:T(8,128)(2,1)S(1)}, bf16[512,768]{1,0:T(8,128)(2,1)}, u32[]{:S(2)}) copy-start(bf16[512,768]{1,0:T(8,128)(2,1)} %mentions_hbm.1) | copy-start | bytes 2359300
  2.5 1.1 %copy-start.1 = (bf16[512,768]{1,0:T(8,128)(2,1)S(1)}, bf16[512,768]{1,0:T(8,128)(2,1)}, u32[]{:S(2)}) copy-start(bf16[512,768]{1,0:T(8,128)(2,1)} %gold_hbm.1) | copy-start | bytes 2359300
  3.6 0.9 %copy-start.2 = (bf16[128,768]{1,0:T(8,128)(2,1)S(1)}, bf16[128,768]{1,0:T(8,128)(2,1)}, u32[]{:S(2)}) copy-start(bf16[128,768]{1,0:T(8,128)(2,1)} %cache_hbm.1) | copy-start | bytes 589828

commit v2 on v1

v2 whole, which is shorter than its diff:
```python
import functools

import jax
import jax.numpy as jnp
from jax import lax
from jax.experimental import pallas as pl
from jax.experimental.pallas import tpu as pltpu
from jax.sharding import PartitionSpec as P

MESH = pl.DeviceIdType.MESH
NEG = -1e30
FLOOR = -1e20
NX, NY, NZ = 4, 4, 8
LEVELS = 32766.0
TINY = 1e-35
PEERS = ((2, 1), (1, 1), (3, 1), (0, 1), (2, 0), (1, 0), (3, 0))
FAR = 4
GROUPS = ((0, 8), (1, 2), (3, 4), (9, 10), (5, 6), (11, 12), (7, 13), (14,), (15,))
ORDER = sum(GROUPS, ())
SLOT = {k: i for i, k in enumerate(ORDER)}
PAIRS = 7
PIECES = 2
IDS, WHOLE = PIECES, -1
EVENTS = (
    ((("y", 0),), (("z", 1), ("z", 2))),
    (),
    ((("z", 3), ("z", 4)), (("y", 1),)),
    ((("y", 2),), (("z", 5), ("z", 6))),
    ((("y", 3),),),
    ((("y", 4),), (("z", 7),)),
    ((("y", 5),),),
    ((("y", 6),),),
    ((("y", 7),),),
)


def place(x, y, z, c):
    return ((y % 2 * NZ + z) * 2 + c, (y // 2) * NX + x)


def kernel(
    mentions_hbm, gold_hbm, gold_ids_hbm, cache_hbm, cache_ids_hbm, loss_ref, grad_ref,
    buf, ids, gids, men, gold, gid, gscore, run, low, u, q, rq, stat, rstat, fac, turned,
    local_sem, zs, zr, ys, yr, cs, cr, qs, qr, ss, sr,
):
    w = lax.axis_index("wide")
    n = lax.axis_index("narrow")
    c = w % 2
    z = (w // 2) % NZ
    y = (n // NX) * 2 + w // (2 * NZ)
    x = n % NX
    rows = buf.shape[2]
    piece = rows // PIECES
    count = men.shape[0]
    blocks = count // 128
    half = count // 2
    part = grad_ref.shape[0]
    way = 1 - 2 * c

    ahead = place(x, y, (z + NZ + way) % NZ, c)
    behind = place(x, y, (z + NZ - way) % NZ, c)
    side = place(x, (y + NY + way) % NY, z, c)
    other_side = place(x, (y + NY - way) % NY, z, c)
    twin = place(x, y, z, 1 - c)

    def peer(dx, dy, sign):
        return place((x + NX + sign * dx) % NX, (y + 2 * dy) % NY, z, c)

    load_c = pltpu.make_async_copy(cache_hbm, buf.at[SLOT[0], c], local_sem.at[0])
    load_i = pltpu.make_async_copy(cache_ids_hbm, ids.at[SLOT[0], c], local_sem.at[1])
    load_n = pltpu.make_async_copy(gold_ids_hbm, gids, local_sem.at[2])
    load_m = pltpu.make_async_copy(mentions_hbm, men, local_sem.at[3])
    load_g = pltpu.make_async_copy(gold_hbm, gold, local_sem.at[4])
    for cp in (load_c, load_i, load_n, load_m, load_g):
        cp.start()

    barrier = pltpu.get_barrier_semaphore()
    sources = [ahead, behind, other_side, twin] + [peer(dx, dy, -1) for dx, dy in PEERS]
    for d in sources:
        pl.semaphore_signal(barrier, inc=1, device_id=d, device_id_type=MESH)

    def moved(what, src, dst, send, recv, index, core, target, own=False):
        if what == IDS:
            source, goal = ids.at[src, core], ids.at[dst, core]
        elif what == WHOLE:
            source, goal = buf.at[src, core], buf.at[dst, core]
        else:
            s = pl.ds(what * piece, piece)
            source, goal = buf.at[src, core, s], buf.at[dst, core, s]
        i = 0 if what == WHOLE else what
        if own:
            source = cache_ids_hbm if what == IDS else cache_hbm
            source = source.at[s] if 0 <= what < PIECES else source
        return pltpu.make_async_remote_copy(
            src_ref=source, dst_ref=goal, send_sem=send.at[index, i], recv_sem=recv.at[index, i],
            device_id=target, device_id_type=MESH)

    def z_copy(what, src, dst, target):
        return moved(what, SLOT[src], SLOT[dst], zs, zr, dst, c, target, own=src == 0)

    def y_copy(what, k):
        return moved(what, SLOT[k], SLOT[8 + k], ys, yr, k, c, side, own=k == 0)

    def twin_copy(what, slot):
        return moved(what, slot, slot, cs, cr, slot, c, twin, own=slot == SLOT[0])

    def twin_arrival(what, slot):
        return moved(what, slot, slot, cs, cr, slot, 1 - c, twin)

    def to_twin(what, slot):
        if what == IDS:
            twin_copy(IDS, slot).start()
        elif what == PIECES - 1:
            twin_copy(WHOLE, slot).start()

    def handle(events):
        for together in events:
            for what in (IDS,) + tuple(range(PIECES)):
                for kind, k in together:
                    if kind == "z":
                        z_copy(what, k, k, ahead).wait_recv()
                        if k <= 5:
                            z_copy(what, k, k + 2, ahead if k % 2 else behind).start()
                        y_copy(what, k).start()
                        to_twin(what, SLOT[k])
                    else:
                        y_copy(what, k).wait_recv()
                        to_twin(what, SLOT[8 + k])

    pl.semaphore_wait(barrier, len(sources))
    for what in (IDS,) + tuple(range(PIECES)):
        z_copy(what, 0, 1, ahead).start()
        z_copy(what, 0, 2, behind).start()
        y_copy(what, 0).start()
        to_twin(what, SLOT[0])

    run[...] = jnp.full(run.shape, FLOOR, jnp.float32)
    low[...] = jnp.zeros(low.shape, jnp.float32)
    u[...] = jnp.zeros(u.shape, jnp.float32)
    fac[...] = jnp.zeros(fac.shape, jnp.float32)
    load_n.wait()
    load_i.wait()
    load_c.wait()
    for b in range(blocks):
        row = jnp.broadcast_to(gids[pl.ds(b, 1), :].astype(jnp.float32), (128, 128))
        gid[pl.ds(b * 128, 128), :] = row.T

    load_m.wait()
    load_g.wait()

    def gold_block(b, _):
        s = pl.ds(pl.multiple_of(b * 128, 128), 128)
        both = men[s, :].astype(jnp.float32) * gold[s, :].astype(jnp.float32)
        score = jnp.broadcast_to(jnp.sum(both, axis=1, keepdims=True), (128, 128))
        gscore[pl.ds(b, 1), :] = score.T[0:1, :]
        return 0

    lax.fori_loop(0, blocks, gold_block, 0)

    def attend(slot, width, first):
        s = pl.ds(first, half)
        block = buf[pl.ds(slot, width)].reshape(2 * width * rows, buf.shape[3])
        scores = lax.dot_general(
            men[s, :], block, (((1,), (1,)), ((), ())), preferred_element_type=jnp.float32
        )
        owner = gid[s, :]
        parts = []
        for i in range(2 * width):
            named = ids[slot + i // 2, i % 2].astype(jnp.float32)
            parts.append(jnp.where(named == owner, NEG, scores[:, rows * i:rows * (i + 1)]))
        before = run[s, :]
        newest = jnp.maximum(before, jnp.max(functools.reduce(jnp.maximum, parts), axis=1, keepdims=True))
        shrink = jnp.exp(before - newest)
        parts = [jnp.exp(t - newest) for t in parts]
        run[s, :] = newest
        low[s, :] = low[s, :] * shrink + functools.reduce(jnp.add, parts)
        weights = jnp.concatenate([t.astype(jnp.bfloat16) for t in parts], axis=1)
        terms = jnp.dot(weights, block, preferred_element_type=jnp.float32)
        for f in range(0, terms.shape[1], 128):
            u[s, f:f + 128] = u[s, f:f + 128] * shrink + terms[:, f:f + 128]

    def twins(slot, width):
        for i in range(width):
            for what in (IDS, WHOLE):
                twin_arrival(what, slot + i).wait_recv()

    def step(j, _):
        for i, events in enumerate(EVENTS[:PAIRS]):
            if events:
                pl.when(j == i)(functools.partial(handle, events))
        twins(2 * j, 2)
        for h in range(2):
            attend(2 * j, 2, h * half)
        return 0

    lax.fori_loop(0, PAIRS, step, 0)

    lane = lax.broadcasted_iota(jnp.int32, (128, 128), 1)

    def settle(first):
        for i in range(half // 128):
            at = pl.multiple_of(first + i * 128, 128)
            s = pl.ds(at, 128)
            b = at // 128
            size = jnp.maximum(jnp.max(jnp.abs(u[s, :]), axis=1, keepdims=True), TINY)
            total = jnp.sum(low[s, :], axis=1, keepdims=True)
            cols = jnp.where(lane == 0, run[s, :], jnp.where(lane == 1, total, size))
            turn = cols.T
            stat[pl.ds(b, 1), :] = turn[0:1, :]
            stat[pl.ds(blocks + b, 1), :] = turn[1:2, :]
            stat[pl.ds(2 * blocks + b, 1), :] = turn[2:3, :]
            q[s, :] = jnp.round(u[s, :] * (LEVELS / size)).astype(jnp.int32).astype(jnp.int16)

    stat_copies, q_copies = [], []
    for e, (dx, dy) in enumerate(PEERS):
        there = peer(dx, dy, 1)
        owner_row = ((n // NX + dy) % 2) * NX + (x + dx) % NX
        first = pl.multiple_of(owner_row * part, part)
        stat_copies.append(pltpu.make_async_remote_copy(
            src_ref=stat, dst_ref=rstat.at[e], send_sem=ss.at[e], recv_sem=sr.at[e],
            device_id=there, device_id_type=MESH))
        q_copies.append(pltpu.make_async_remote_copy(
            src_ref=q.at[pl.ds(first, part)], dst_ref=rq.at[e], send_sem=qs.at[e], recv_sem=qr.at[e],
            device_id=there, device_id_type=MESH))

    far_rows = pl.multiple_of((1 - n // NX) * half, half)
    near_rows = pl.multiple_of((n // NX) * half, half)
    for i in range(PAIRS, len(GROUPS)):
        slot, width = SLOT[GROUPS[i][0]], len(GROUPS[i])
        handle(EVENTS[i])
        twins(slot, width)
        attend(slot, width, far_rows)
        if i < len(GROUPS) - 1:
            attend(slot, width, near_rows)
    settle(far_rows)
    for cp in q_copies[:FAR]:
        cp.start()
    attend(SLOT[15], 1, near_rows)
    settle(near_rows)
    for cp in stat_copies:
        cp.start()
    for cp in q_copies[FAR:]:
        cp.start()
    for cp in stat_copies:
        cp.wait_recv()

    golds = gscore[...]
    tops = [stat[0:blocks, :]] + [rstat[e, 0:blocks, :] for e in range(len(PEERS))]
    sums = [stat[blocks:2 * blocks, :]] + [rstat[e, blocks:2 * blocks, :] for e in range(len(PEERS))]
    highest = golds
    for t in tops:
        highest = jnp.maximum(highest, t)
    whole = jnp.exp(golds - highest)
    for t, t_sum in zip(tops, sums):
        whole = whole + t_sum * jnp.exp(t - highest)
    lse = highest + jnp.log(whole)
    loss_ref[...] = lse - golds
    gscore[...] = jnp.exp(golds - lse) - 1.0
    run[0:blocks, :] = lse

    mine = (n * part) // 128
    row = pl.ds(mine, 1)
    my_lse = run[row, :]
    fac[0:1, :] = jnp.exp(stat[row, :] - my_lse)
    fac[1:2, :] = gscore[row, :]
    for e in range(len(PEERS)):
        size = rstat[e, pl.ds(2 * blocks + mine, 1), :] * (1.0 / LEVELS)
        fac[2 + e:3 + e, :] = size * jnp.exp(rstat[e, row, :] - my_lse)
    turned[...] = fac[...].T
    f = turned[pl.ds(pl.multiple_of((n * part) % 128, part), part), :]
    own = pl.ds(pl.multiple_of(n * part, part), part)
    grad_ref[...] = u[own, :] * f[:, 0:1] + gold[own, :].astype(jnp.float32) * f[:, 1:2]
    for what in (IDS,) + tuple(range(PIECES)):
        for k in range(1, 8):
            z_copy(what, k, k, ahead).wait_send()
        for k in range(8):
            y_copy(what, k).wait_send()
    for what in (IDS, WHOLE):
        for k in range(16):
            twin_copy(what, k).wait_send()
    for e in range(len(PEERS)):
        q_copies[e].wait_recv()
        grad_ref[...] += rq[e].astype(jnp.int32).astype(jnp.float32) * f[:, 2 + e:3 + e]

    for cp in stat_copies + q_copies:
        cp.wait_send()


def per_device(mentions, gold_vectors, gold_ids, cache, cache_ids):
    count, features = mentions.shape
    rows = cache.shape[0]
    blocks = count // 128
    part = count // 8
    near = len(PEERS)
    any_ = pl.BlockSpec(memory_space=pl.ANY)
    vmem = pl.BlockSpec(memory_space=pltpu.VMEM)
    dma = pltpu.SemaphoreType.DMA
    loss, grad = pl.pallas_call(
        kernel,
        out_shape=(
            jax.ShapeDtypeStruct((blocks, 128), jnp.float32),
            jax.ShapeDtypeStruct((part, features), jnp.float32),
        ),
        in_specs=[any_] * 5,
        out_specs=(vmem, vmem),
        scratch_shapes=[
            pltpu.VMEM((16, 2, rows, features), jnp.bfloat16),
            pltpu.VMEM((16, 2, 1, rows), jnp.int32),
            pltpu.VMEM((blocks, 128), jnp.int32),
            pltpu.VMEM((count, features), jnp.bfloat16),
            pltpu.VMEM((count, features), jnp.bfloat16),
            pltpu.VMEM((count, 128), jnp.float32),
            pltpu.VMEM((blocks, 128), jnp.float32),
            pltpu.VMEM((count, 128), jnp.float32),
            pltpu.VMEM((count, 128), jnp.float32),
            pltpu.VMEM((count, features), jnp.float32),
            pltpu.VMEM((count, features), jnp.int16),
            pltpu.VMEM((near, part, features), jnp.int16),
            pltpu.VMEM((4 * blocks, 128), jnp.float32),
            pltpu.VMEM((near, 4 * blocks, 128), jnp.float32),
            pltpu.VMEM((128, 128), jnp.float32),
            pltpu.VMEM((128, 128), jnp.float32),
            dma((5,)),
            dma((8, PIECES + 1)),
            dma((8, PIECES + 1)),
            dma((8, PIECES + 1)),
            dma((8, PIECES + 1)),
            dma((16, PIECES + 1)),
            dma((16, PIECES + 1)),
            dma((near,)),
            dma((near,)),
            dma((near,)),
            dma((near,)),
        ],
        compiler_params=pltpu.CompilerParams(
            collective_id=0, has_side_effects=True, vmem_limit_bytes=55000 * 1024
        ),
        name="linking",
    )(mentions, gold_vectors, gold_ids.reshape(blocks, 128), cache, cache_ids.reshape(1, rows))
    return loss.reshape(count), grad


def solution(mesh):
    in_specs = (
        P("wide", None),
        P("wide", None),
        P("wide"),
        P(("wide", "narrow"), None),
        P(("wide", "narrow")),
    )
    out_specs = (P("wide"), P(("wide", "narrow"), None))
    return jax.shard_map(
        per_device, mesh=mesh, in_specs=in_specs, out_specs=out_specs, check_vma=False
    )
```

time: 73.5 us -> 57.3 us (0.78)
  Pallas kernels: 67.5 us -> 54.6 us
  local copies, waits for them, and re-layouts: 5.12 us -> 1.93 us
    pallas_call x1, Pallas kernels: 67.5 us -> 54.6 us  [per_device(): pl.pallas_call(kernel, out_shape=(jax.ShapeDtypeStruct((blocks, 128), jnp...]
    unnamed x12 -> x6, local copies, waits for them, and re-layouts: 5.12 us -> 1.93 us
where the time goes in v2:
time: 57.3 us; the launch traced here: 57.2 us
  Pallas kernels  54.6 us (95%)
  local copies, waits for them, and re-layouts  1.93 us (3%)
  between operations  0.66 us (1%)
    pallas_call x1, Pallas kernels, per_device(): pl.pallas_call(kernel, out_shape=(jax.ShapeDtypeStruct((blocks, 128), jnp...  54.6 us
    unnamed x6, local copies, waits for them, and re-layouts  1.93 us

profile of v2, /device:TPU:1, one launch (start us, length us, event | category | flops | bytes accessed | tf_op | source)
XLA Modules:
  0.0 57.2 jit_solution(12797119208308149058)
XLA Ops:
  0.6 0.0 copy-start
  0.6 0.0 copy-start.1
  0.7 0.7 %copy-done = s32[512]{0:T(512)S(1)} copy-done((s32[512]{0:T(512)S(1)}, s32[512]{0:T(512)}, u32[]{:S(2)}) %copy-start) | copy-done | bytes 2072
  1.3 0.0 copy-done.1
  1.3 54.6 %linking.1 = (f32[4,128]{1,0:T(4,128)S(1)}, f32[64,768]{1,0:T(8,128)S(1)}) custom-call(bf16[512,768]{1,0:T(8,128)(2,1)} %mentions_hbm.1, bf16[512,768]{1,0:T(8,128)(2,1)} %gold_hbm.1, s32[4,128]{1,0:T(4,128)S(1)} %bitcast.3, bf16[128,768]{1,0:T(8,128)(2,1)} %cache_hbm.1, s32[1,128]{1,0:T(1,128)S(1)} %bitcast.5), custom_call_target="tpu_custom_call" | custom-call | tf_op jit(solution)/shard_map/linking/pallas_call | solution.py:298
  55.9 0.6 %copy.9 = f32[512]{0:T(512)} copy(f32[512]{0:T(512)S(1)} %bitcast.4) | data formatting | bytes 4096
  56.5 0.7 %copy.10 = f32[64,768]{1,0:T(8,128)} copy(f32[64,768]{1,0:T(8,128)S(1)} %get-tuple-element.9) | data formatting | bytes 393216
Async XLA Ops:
  0.6 0.7 %copy-start = (s32[512]{0:T(512)S(1)}, s32[512]{0:T(512)}, u32[]{:S(2)}) copy-start(s32[512]{0:T(512)} %param.7) | copy-start | bytes 6148
  0.6 0.7 %copy-start.1 = (s32[128]{0:T(128)S(1)}, s32[128]{0:T(128)}, u32[]{:S(2)}) copy-start(s32[128]{0:T(128)} %param.9) | copy-start | bytes 1540

commit v3 on v2

--- a/solution.py
+++ b/solution.py
@@ -26,11 +26,11 @@
     (),
     ((("z", 3), ("z", 4)), (("y", 1),)),
     ((("y", 2),), (("z", 5), ("z", 6))),
-    ((("y", 3),),),
-    ((("y", 4),), (("z", 7),)),
-    ((("y", 5),),),
-    ((("y", 6),),),
-    ((("y", 7),),),
+    ((("y", 3),), (("y", 4),)),
+    ((("z", 7),),),
+    ((("y", 5),), (("y", 6),), (("y", 7),)),
+    (),
+    (),
 )
 
 
@@ -110,8 +110,8 @@
     def to_twin(what, slot):
         if what == IDS:
             twin_copy(IDS, slot).start()
-        elif what == PIECES - 1:
-            twin_copy(WHOLE, slot).start()
+        else:
+            twin_copy(what, slot).start()
 
     def handle(events):
         for together in events:
@@ -181,7 +181,7 @@
 
     def twins(slot, width):
         for i in range(width):
-            for what in (IDS, WHOLE):
+            for what in (IDS,) + tuple(range(PIECES)):
                 twin_arrival(what, slot + i).wait_recv()
 
     def step(j, _):
@@ -198,6 +198,7 @@
     lane = lax.broadcasted_iota(jnp.int32, (128, 128), 1)
 
     def settle(first):
+        sizes = []
         for i in range(half // 128):
             at = pl.multiple_of(first + i * 128, 128)
             s = pl.ds(at, 128)
@@ -209,6 +210,11 @@
             stat[pl.ds(b, 1), :] = turn[0:1, :]
             stat[pl.ds(blocks + b, 1), :] = turn[1:2, :]
             stat[pl.ds(2 * blocks + b, 1), :] = turn[2:3, :]
+            sizes.append((s, size))
+        return sizes
+
+    def quantize(sizes):
+        for s, size in sizes:
             q[s, :] = jnp.round(u[s, :] * (LEVELS / size)).astype(jnp.int32).astype(jnp.int16)
 
     stat_copies, q_copies = [], []
@@ -232,13 +238,14 @@
         attend(slot, width, far_rows)
         if i < len(GROUPS) - 1:
             attend(slot, width, near_rows)
-    settle(far_rows)
+    quantize(settle(far_rows))
     for cp in q_copies[:FAR]:
         cp.start()
     attend(SLOT[15], 1, near_rows)
-    settle(near_rows)
+    sizes = settle(near_rows)
     for cp in stat_copies:
         cp.start()
+    quantize(sizes)
     for cp in q_copies[FAR:]:
         cp.start()
     for cp in stat_copies:
@@ -275,7 +282,7 @@
             z_copy(what, k, k, ahead).wait_send()
         for k in range(8):
             y_copy(what, k).wait_send()
-    for what in (IDS, WHOLE):
+    for what in (IDS,) + tuple(range(PIECES)):
         for k in range(16):
             twin_copy(what, k).wait_send()
     for e in range(len(PEERS)):

time: 57.3 us -> 53.9 us (0.941)
  Pallas kernels: 54.6 us -> 51.2 us
    pallas_call x1, Pallas kernels: 54.6 us -> 51.2 us  [per_device(): pl.pallas_call(kernel, out_shape=(jax.ShapeDtypeStruct((blocks, 128), jnp...]
where the time goes in v3:
time: 53.9 us; the launch traced here: 53.7 us
  Pallas kernels  51.2 us (95%)
  local copies, waits for them, and re-layouts  1.93 us (4%)
  between operations  0.66 us (1%)
    pallas_call x1, Pallas kernels, per_device(): pl.pallas_call(kernel, out_shape=(jax.ShapeDtypeStruct((blocks, 128), jnp...  51.2 us
    unnamed x6, local copies, waits for them, and re-layouts  1.93 us

profile of v3, /device:TPU:1, one launch (start us, length us, event | category | flops | bytes accessed | tf_op | source)
XLA Modules:
  0.0 53.7 jit_solution(5160305872779773721)
XLA Ops:
  0.6 0.0 copy-start
  0.6 0.0 copy-start.1
  0.7 0.7 %copy-done = s32[512]{0:T(512)S(1)} copy-done((s32[512]{0:T(512)S(1)}, s32[512]{0:T(512)}, u32[]{:S(2)}) %copy-start) | copy-done | bytes 2072
  1.3 0.0 copy-done.1
  1.3 51.2 %linking.1 = (f32[4,128]{1,0:T(4,128)S(1)}, f32[64,768]{1,0:T(8,128)S(1)}) custom-call(bf16[512,768]{1,0:T(8,128)(2,1)} %mentions_hbm.1, bf16[512,768]{1,0:T(8,128)(2,1)} %gold_hbm.1, s32[4,128]{1,0:T(4,128)S(1)} %bitcast.3, bf16[128,768]{1,0:T(8,128)(2,1)} %cache_hbm.1, s32[1,128]{1,0:T(1,128)S(1)} %bitcast.5), custom_call_target="tpu_custom_call" | custom-call | tf_op jit(solution)/shard_map/linking/pallas_call | solution.py:305
  52.5 0.6 %copy.9 = f32[512]{0:T(512)} copy(f32[512]{0:T(512)S(1)} %bitcast.4) | data formatting | bytes 4096
  53.1 0.7 %copy.10 = f32[64,768]{1,0:T(8,128)} copy(f32[64,768]{1,0:T(8,128)S(1)} %get-tuple-element.9) | data formatting | bytes 393216
Async XLA Ops:
  0.6 0.7 %copy-start = (s32[512]{0:T(512)S(1)}, s32[512]{0:T(512)}, u32[]{:S(2)}) copy-start(s32[512]{0:T(512)} %param.7) | copy-start | bytes 6148
  0.6 0.7 %copy-start.1 = (s32[128]{0:T(128)S(1)}, s32[128]{0:T(128)}, u32[]{:S(2)}) copy-start(s32[128]{0:T(128)} %param.9) | copy-start | bytes 1540

commit v4 on v3

--- a/solution.py
+++ b/solution.py
@@ -24,8 +24,8 @@
 EVENTS = (
     ((("y", 0),), (("z", 1), ("z", 2))),
     (),
-    ((("z", 3), ("z", 4)), (("y", 1),)),
-    ((("y", 2),), (("z", 5), ("z", 6))),
+    ((("z", 3), ("z", 4)), (("y", 1),), (("y", 2),)),
+    ((("z", 5), ("z", 6)),),
     ((("y", 3),), (("y", 4),)),
     ((("z", 7),),),
     ((("y", 5),), (("y", 6),), (("y", 7),)),
@@ -66,6 +66,11 @@
     def peer(dx, dy, sign):
         return place((x + NX + sign * dx) % NX, (y + 2 * dy) % NY, z, c)
 
+    barrier = pltpu.get_barrier_semaphore()
+    sources = [peer(dx, dy, -1) for dx, dy in PEERS] + [ahead, behind, other_side, twin]
+    for d in sources:
+        pl.semaphore_signal(barrier, inc=1, device_id=d, device_id_type=MESH)
+
     load_c = pltpu.make_async_copy(cache_hbm, buf.at[SLOT[0], c], local_sem.at[0])
     load_i = pltpu.make_async_copy(cache_ids_hbm, ids.at[SLOT[0], c], local_sem.at[1])
     load_n = pltpu.make_async_copy(gold_ids_hbm, gids, local_sem.at[2])
@@ -73,11 +78,6 @@
     load_g = pltpu.make_async_copy(gold_hbm, gold, local_sem.at[4])
     for cp in (load_c, load_i, load_n, load_m, load_g):
         cp.start()
-
-    barrier = pltpu.get_barrier_semaphore()
-    sources = [ahead, behind, other_side, twin] + [peer(dx, dy, -1) for dx, dy in PEERS]
-    for d in sources:
-        pl.semaphore_signal(barrier, inc=1, device_id=d, device_id_type=MESH)
 
     def moved(what, src, dst, send, recv, index, core, target, own=False):
         if what == IDS:

time: 53.9 us -> 53.8 us (level)
  no operation moved by 1% of the time
where the time goes in v4:
time: 53.8 us; the launch traced here: 53.3 us
  Pallas kernels  50.7 us (94%)
  local copies, waits for them, and re-layouts  1.93 us (4%)
  between operations  0.66 us (1%)
    pallas_call x1, Pallas kernels, per_device(): pl.pallas_call(kernel, out_shape=(jax.ShapeDtypeStruct((blocks, 128), jnp...  50.7 us
    unnamed x6, local copies, waits for them, and re-layouts  1.93 us

profile of v4, /device:TPU:1, one launch (start us, length us, event | category | flops | bytes accessed | tf_op | source)
XLA Modules:
  0.0 53.3 jit_solution(1087150669212182114)
XLA Ops:
  0.6 0.0 copy-start
  0.6 0.0 copy-start.1
  0.7 0.7 %copy-done = s32[512]{0:T(512)S(1)} copy-done((s32[512]{0:T(512)S(1)}, s32[512]{0:T(512)}, u32[]{:S(2)}) %copy-start) | copy-done | bytes 2072
  1.3 0.0 copy-done.1
  1.3 50.7 %linking.1 = (f32[4,128]{1,0:T(4,128)S(1)}, f32[64,768]{1,0:T(8,128)S(1)}) custom-call(bf16[512,768]{1,0:T(8,128)(2,1)} %mentions_hbm.1, bf16[512,768]{1,0:T(8,128)(2,1)} %gold_hbm.1, s32[4,128]{1,0:T(4,128)S(1)} %bitcast.3, bf16[128,768]{1,0:T(8,128)(2,1)} %cache_hbm.1, s32[1,128]{1,0:T(1,128)S(1)} %bitcast.5), custom_call_target="tpu_custom_call" | custom-call | tf_op jit(solution)/shard_map/linking/pallas_call | solution.py:305
  52.0 0.6 %copy.9 = f32[512]{0:T(512)} copy(f32[512]{0:T(512)S(1)} %bitcast.4) | data formatting | bytes 4096
  52.6 0.7 %copy.10 = f32[64,768]{1,0:T(8,128)} copy(f32[64,768]{1,0:T(8,128)S(1)} %get-tuple-element.9) | data formatting | bytes 393216
Async XLA Ops:
  0.6 0.7 %copy-start = (s32[512]{0:T(512)S(1)}, s32[512]{0:T(512)}, u32[]{:S(2)}) copy-start(s32[512]{0:T(512)} %param.7) | copy-start | bytes 6148
  0.6 0.7 %copy-start.1 = (s32[128]{0:T(128)S(1)}, s32[128]{0:T(128)}, u32[]{:S(2)}) copy-start(s32[128]{0:T(128)} %param.9) | copy-start | bytes 1540

commit v5 on v4

--- a/solution.py
+++ b/solution.py
@@ -12,7 +12,7 @@
 FLOOR = -1e20
 NX, NY, NZ = 4, 4, 8
 LEVELS = 32766.0
-TINY = 1e-35
+TINY = 1e-30
 PEERS = ((2, 1), (1, 1), (3, 1), (0, 1), (2, 0), (1, 0), (3, 0))
 FAR = 4
 GROUPS = ((0, 8), (1, 2), (3, 4), (9, 10), (5, 6), (11, 12), (7, 13), (14,), (15,))
@@ -24,11 +24,11 @@
 EVENTS = (
     ((("y", 0),), (("z", 1), ("z", 2))),
     (),
-    ((("z", 3), ("z", 4)), (("y", 1),), (("y", 2),)),
+    ((("z", 3), ("z", 4)), (("y", 1), ("y", 2))),
     ((("z", 5), ("z", 6)),),
-    ((("y", 3),), (("y", 4),)),
+    ((("y", 3), ("y", 4)),),
     ((("z", 7),),),
-    ((("y", 5),), (("y", 6),), (("y", 7),)),
+    ((("y", 5), ("y", 6)), (("y", 7),)),
     (),
     (),
 )

time: 53.8 us -> 53.8 us (level)
  no operation moved by 1% of the time
where the time goes in v5:
time: 53.8 us; the launch traced here: 53.3 us
  Pallas kernels  50.7 us (94%)
  local copies, waits for them, and re-layouts  1.93 us (4%)
  between operations  0.66 us (1%)
    pallas_call x1, Pallas kernels, per_device(): pl.pallas_call(kernel, out_shape=(jax.ShapeDtypeStruct((blocks, 128), jnp...  50.7 us
    unnamed x6, local copies, waits for them, and re-layouts  1.93 us

profile of v5, /device:TPU:1, one launch (start us, length us, event | category | flops | bytes accessed | tf_op | source)
XLA Modules:
  0.0 53.3 jit_solution(465471324002872116)
XLA Ops:
  0.6 0.0 copy-start
  0.6 0.0 copy-start.1
  0.7 0.7 %copy-done = s32[512]{0:T(512)S(1)} copy-done((s32[512]{0:T(512)S(1)}, s32[512]{0:T(512)}, u32[]{:S(2)}) %copy-start) | copy-done | bytes 2072
  1.3 0.0 copy-done.1
  1.3 50.7 %linking.1 = (f32[4,128]{1,0:T(4,128)S(1)}, f32[64,768]{1,0:T(8,128)S(1)}) custom-call(bf16[512,768]{1,0:T(8,128)(2,1)} %mentions_hbm.1, bf16[512,768]{1,0:T(8,128)(2,1)} %gold_hbm.1, s32[4,128]{1,0:T(4,128)S(1)} %bitcast.3, bf16[128,768]{1,0:T(8,128)(2,1)} %cache_hbm.1, s32[1,128]{1,0:T(1,128)S(1)} %bitcast.5), custom_call_target="tpu_custom_call" | custom-call | tf_op jit(solution)/shard_map/linking/pallas_call | solution.py:305
  52.0 0.6 %copy.9 = f32[512]{0:T(512)} copy(f32[512]{0:T(512)S(1)} %bitcast.4) | data formatting | bytes 4096
  52.6 0.7 %copy.10 = f32[64,768]{1,0:T(8,128)} copy(f32[64,768]{1,0:T(8,128)S(1)} %get-tuple-element.9) | data formatting | bytes 393216
Async XLA Ops:
  0.6 0.7 %copy-start = (s32[512]{0:T(512)S(1)}, s32[512]{0:T(512)}, u32[]{:S(2)}) copy-start(s32[512]{0:T(512)} %param.7) | copy-start | bytes 6148
  0.6 0.7 %copy-start.1 = (s32[128]{0:T(128)S(1)}, s32[128]{0:T(128)}, u32[]{:S(2)}) copy-start(s32[128]{0:T(128)} %param.9) | copy-start | bytes 1540
